TPU v7x, 32 devices: a whole 2x2x4 slice. The times are simulated.
32 devices in a mesh: blk: 8 (over z, x), win: 4 (over y, core).
Axes of the slice: x: 2, y: 2, z: 4, core: 2. Of those that a mesh axis runs over, the one named last changes fastest.
Arguments:
- samples: bfloat16 [1024, 32, 2048], P('blk', 'win'), may hold values from -6 to 6
- pair_offsets: int32 [24], P('blk'), may hold values from 0 to 4, as said below
- pair_count: int32 [8], P('blk'), may hold values from 1 to 3
Outputs:
- cross_spectra: bfloat16 [24, 128, 2, 128, 128], P('blk', 'win')
Inputs may be any that keep to these rules, and one draw needn't show every extreme that they name: `pair_offsets`: entry w * 3 + s belongs to worker w. The live slots of a worker (s below its count) hold different offsets, with w + offset below the number of blocks; the other slots hold 0.
All inputs are finite; a program needn't handle non-finite values.
Results may differ from a plain program's by a relative error of at most 0.0068.
Values may be sent and summed in bfloat16 or wider, within the bound.
A program may use at most 64 MiB of HBM per device.

v0:
```python
import math
import jax
import jax.numpy as jnp
from jax import lax
from jax.sharding import PartitionSpec as P

BINS = 128
BIN0 = 32
SMOOTH = 4
OFFSET = 4
water_level = 0.1
epsilon = 1e-06


def shifted(block, axis, distance):
    devices = range(lax.axis_size(axis))
    route = [(i - distance, i) for i in devices if i - distance in devices]
    return lax.ppermute(block, axis, route)


def dft_table(length):
    sample_idx = jnp.arange(length, dtype=jnp.int32)
    bin_freqs = BIN0 + jnp.arange(BINS, dtype=jnp.int32)
    phases = sample_idx[:, None] * bin_freqs[None, :] % length
    angles = phases.astype(jnp.float32) * (2.0 * math.pi / length)
    window_taper = 0.5 - 0.5 * jnp.cos(
        (sample_idx.astype(jnp.float32) + 0.5) * (2.0 * math.pi / length)
    )
    cosines = window_taper[:, None] * jnp.cos(angles)
    sines = -window_taper[:, None] * jnp.sin(angles)
    return jnp.concatenate([cosines, sines], axis=1).astype(jnp.bfloat16)


def band_weights():
    bin_index = jnp.arange(BINS, dtype=jnp.int32)
    inside = (jnp.abs(bin_index[:, None] - bin_index[None, :]) <= SMOOTH).astype(jnp.float32)
    return inside / jnp.sum(inside, axis=0, keepdims=True)


def whiten_spectrum(spectrum, weights):
    energy = spectrum[:, 0] * spectrum[:, 0] + spectrum[:, 1] * spectrum[:, 1]
    smoothed = jnp.einsum("wjc,jb->wbc", energy, weights, precision=lax.Precision.HIGHEST)
    average = jnp.mean(energy, axis=1, keepdims=True)
    factor = lax.rsqrt(smoothed + water_level * average + epsilon)
    return (spectrum * factor[:, None]).astype(jnp.bfloat16)


def cross_pair(left_side, partner, windows):
    right_side = partner.reshape(2 * windows, partner.shape[2], partner.shape[3])
    product = lax.dot_general(
        left_side, right_side, (((1,), (0,)), ((2,), (1,))), preferred_element_type=jnp.float32
    )
    return product * (1.0 / windows)


def shards(samples, pair_offsets, pair_count):
    channels, win_dev, length = samples.shape
    table = dft_table(length)
    weights = band_weights()
    spectrum = jnp.einsum("cwt,tk->wkc", samples, table, preferred_element_type=jnp.float32)
    whitened = whiten_spectrum(spectrum.reshape(win_dev, 2, BINS, channels), weights)
    by_bins = lax.all_to_all(whitened, "win", split_axis=2, concat_axis=0, tiled=True)
    windows = by_bins.shape[0]
    bins_dev = by_bins.shape[2]
    swapped = jnp.stack([by_bins[:, 1], -by_bins[:, 0]], axis=1)
    left_side = jnp.stack([by_bins, swapped], axis=0).reshape(2, 2 * windows, bins_dev, channels)
    neighbours = [by_bins]
    for distance in range(1, OFFSET + 1):
        neighbours.append(shifted(by_bins, "blk", -distance))
    nearby = jnp.stack(neighbours, axis=0)
    live_count = pair_count[0]
    slot_total = pair_offsets.shape[0]
    results = []
    for slot_rank in range(slot_total):
        partner = lax.dynamic_index_in_dim(nearby, pair_offsets[slot_rank], 0, keepdims=False)
        value = cross_pair(left_side, partner, windows)
        results.append(
            jnp.where(slot_rank < live_count, value, jnp.zeros_like(value)).astype(jnp.bfloat16)
        )
    cross_spectra = jnp.stack(results, axis=0)
    return cross_spectra


def solution(mesh):
    in_specs = (P("blk", "win", None), P("blk"), P("blk"))
    out_specs = P("blk", "win", None, None, None)
    return jax.shard_map(shards, mesh=mesh, in_specs=in_specs, out_specs=out_specs, check_vma=False)
```

profile of v0, /device:TPU:0, one launch (start us, length us, event | category | flops | bytes accessed | tf_op | source)
XLA Modules:
  0.0 109.8 jit_solution(9315533526000073080)
XLA Ops:
  0.0 0.1 convert_reduce_fusion
  0.1 0.1 multiply_subtract_fusion
  0.2 4.5 %multiply_convert_fusion.2 = (bf16[2048,128]{0,1:T(8,128)(2,1)S(1)}, bf16[2048,128]{0,1:T(8,128)(2,1)S(1)}) fusion(s32[128]{0:T(128)S(1)} %iota_add_fusion, f32[2048]{0:T(1024)S(1)} %get-tuple-element.15, f32[2048]{0:T(1024)S(1)} %get-tuple-element.16), kind=kLoop, calls=%fused_computation.25 | loop fusion | flops 4718592 | bytes 1065472 | tf_op jit(solution)/shard_map/convert
  4.7 7.1 %fusion = f32[256,128,8]{1,0,2:T(8,128)S(1)} fusion(bf16[128,8,2048]{2,1,0:T(8,128)(2,1)} %param.3, bf16[2048,128]{0,1:T(8,128)(2,1)S(1)} %get-tuple-element.14, bf16[2048,128]{0,1:T(8,128)(2,1)S(1)} %get-tuple-element.13), kind=kOutput, calls=%fused_computation.1 | convolution fusion | flops 1075838976 | bytes 6291456 | tf_op jit(solution)/shard_map/cwt,tk->wkc/dot_general | solution.py:60
  11.9 0.1 fusion.18
  12.0 0.0 copy-start
  12.0 0.6 fusion.7
  12.7 0.1 multiply_convert_fusion
  12.8 1.3 %copy.15 = bf16[8,2,128,128]{3,1,0,2:T(2,128)(2,1)} copy(bf16[8,2,128,128]{3,2,1,0:T(8,128)(2,1)S(1)} %multiply_convert_fusion) | data formatting | bytes 1048576 | tf_op jit(solution)/shard_map/convert_element_type | solution.py:45
  14.1 4.2 %all-to-all-start = ((bf16[8,2,128,128]{3,1,0,2:T(2,128)(2,1)}), bf16[8,2,128,128]{3,1,0,2:T(2,128)(2,1)S(1)}, u32[]{:S(2)}, u32[]{:S(2)}) async-start(bf16[8,2,128,128]{3,1,0,2:T(2,128)(2,1)} %copy.15), calls=%async_computation | async-start | bytes 1048576 | tf_op jit(solution)/shard_map/all_to_all | solution.py:62
  18.3 0.0 copy-done
  18.3 0.7 fusion.31
  25.2 1.9 %all-to-all-done = bf16[8,2,128,128]{3,1,0,2:T(2,128)(2,1)S(1)} async-done(((bf16[8,2,128,128]{3,1,0,2:T(2,128)(2,1)}), bf16[8,2,128,128]{3,1,0,2:T(2,128)(2,1)S(1)}, u32[]{:S(2)}, u32[]{:S(2)}) %all-to-all-start) | async-done | bytes 524320 | tf_op jit(solution)/shard_map/all_to_all | solution.py:62
  27.2 0.5 copy.16
  27.7 1.3 %collective-permute-start.2 = (bf16[32,2,32,128]{3,1,0,2:T(2,128)(2,1)S(1)}, bf16[32,2,32,128]{3,1,0,2:T(2,128)(2,1)S(1)}, u32[]{:S(2)}, u32[]{:S(2)}) collective-permute-start(bf16[32,2,32,128]{3,1,0,2:T(2,128)(2,1)S(1)} %bitcast.62), channel_id=1, source_target_pairs={{12,0},{16,4},{20,8},{24,12},{28,16},{13,1},{17,5},{21,9},{25,13},... | collective-permute-start | bytes 1572872 | tf_op jit(solution)/shard_map/ppermute | solution.py:18
  29.0 1.3 %collective-permute-start.1 = (bf16[32,2,32,128]{3,1,0,2:T(2,128)(2,1)S(1)}, bf16[32,2,32,128]{3,1,0,2:T(2,128)(2,1)S(1)}, u32[]{:S(2)}, u32[]{:S(2)}) collective-permute-start(bf16[32,2,32,128]{3,1,0,2:T(2,128)(2,1)S(1)} %bitcast.63), channel_id=1, source_target_pairs={{8,0},{12,4},{16,8},{20,12},{24,16},{28,20},{9,1},{13,5},{17,9},{2... | collective-permute-start | bytes 1572872 | tf_op jit(solution)/shard_map/ppermute | solution.py:18
  30.3 1.3 %collective-permute-start = (bf16[32,2,32,128]{3,1,0,2:T(2,128)(2,1)S(1)}, bf16[32,2,32,128]{3,1,0,2:T(2,128)(2,1)S(1)}, u32[]{:S(2)}, u32[]{:S(2)}) collective-permute-start(bf16[32,2,32,128]{3,1,0,2:T(2,128)(2,1)S(1)} %bitcast.64), channel_id=1, source_target_pairs={{4,0},{8,4},{12,8},{16,12},{20,16},{24,20},{28,24},{5,1},{9,5},{13... | collective-permute-start | bytes 1572872 | tf_op jit(solution)/shard_map/ppermute | solution.py:18
  31.6 1.5 %collective-permute-start.3 = (bf16[32,2,32,128]{3,1,0,2:T(2,128)(2,1)S(1)}, bf16[32,2,32,128]{3,1,0,2:T(2,128)(2,1)S(1)}, u32[]{:S(2)}, u32[]{:S(2)}) collective-permute-start(bf16[32,2,32,128]{3,1,0,2:T(2,128)(2,1)S(1)} %bitcast.65), channel_id=1, source_target_pairs={{16,0},{20,4},{24,8},{28,12},{17,1},{21,5},{25,9},{29,13},{18,2},{... | collective-permute-start | bytes 1572872 | tf_op jit(solution)/shard_map/ppermute | solution.py:18
  33.1 0.9 fusion.30
  34.1 0.4 constant_dynamic-update-slice_fusion
  34.5 1.2 %pad_maximum_fusion.2 = bf16[32,2,32,128]{3,1,0,2:T(2,128)(2,1)S(1)} fusion(bf16[32,1,32,128]{3,1,0,2:T(2,128)(2,1)S(1)} %get-tuple-element.9, bf16[32,1,32,128]{3,1,0,2:T(2,128)(2,1)S(1)} %get-tuple-element.8), kind=kLoop, calls=%fused_computation.33 | loop fusion | flops 1048576 | bytes 1048576 | tf_op jit(solution)/shard_map/stack | solution.py:65
  35.7 20.0 %collective-permute-done = bf16[32,2,32,128]{3,1,0,2:T(2,128)(2,1)S(1)} collective-permute-done((bf16[32,2,32,128]{3,1,0,2:T(2,128)(2,1)S(1)}, bf16[32,2,32,128]{3,1,0,2:T(2,128)(2,1)S(1)}, u32[]{:S(2)}, u32[]{:S(2)}) %collective-permute-start) | collective-permute-done | bytes 524320 | tf_op jit(solution)/shard_map/ppermute | solution.py:18
  55.7 0.5 bitcast_dynamic-update-slice_fusion.3
  56.2 0.0 collective-permute-done.1
  56.3 0.5 bitcast_dynamic-update-slice_fusion.2
  56.8 0.0 collective-permute-done.2
  56.8 0.5 bitcast_dynamic-update-slice_fusion.1
  57.3 44.6 %collective-permute-done.3 = bf16[32,2,32,128]{3,1,0,2:T(2,128)(2,1)S(1)} collective-permute-done((bf16[32,2,32,128]{3,1,0,2:T(2,128)(2,1)S(1)}, bf16[32,2,32,128]{3,1,0,2:T(2,128)(2,1)S(1)}, u32[]{:S(2)}, u32[]{:S(2)}) %collective-permute-start.3) | collective-permute-done | bytes 524320 | tf_op jit(solution)/shard_map/ppermute | solution.py:18
  101.8 0.5 bitcast_dynamic-update-slice_fusion
  102.3 1.5 %constant_dynamic-slice_fusion.2 = (bf16[1,32,2,32,128]{4,2,1,3,0:T(2,128)(2,1)S(1)}, bf16[1,32,2,32,128]{4,2,1,3,0:T(2,128)(2,1)S(1)}, bf16[1,32,2,32,128]{4,2,1,3,0:T(2,128)(2,1)S(1)}) fusion(bf16[5,32,2,32,128]{4,2,1,3,0:T(2,128)(2,1)S(1)} %bitcast_dynamic-update-slice_fusion, s32[]{:T(128)S(6)} %select_n.41, s32[]{:T(128)S(6)} %select_n.47, s32[]{:T(128)S(6)} %select_n.44), kind=kLoop, calls=%fused_computation.52 | loop fusion | bytes 3145740 | tf_op jit(solution)/shard_map/jit(dynamic_index_in_dim)/dynamic_slice | solution.py:75
  103.8 0.9 fusion.4
  104.7 0.9 fusion.2
  105.7 0.9 fusion.3
  106.6 3.2 %pad_maximum_fusion = bf16[3,32,2,128,128]{4,3,2,1,0:T(8,128)(2,1)} fusion(bf16[1,32,2,128,128]{4,3,2,1,0:T(8,128)(2,1)S(1)} %fusion.4, bf16[1,32,2,128,128]{4,3,2,1,0:T(8,128)(2,1)S(1)} %fusion.3, bf16[1,32,2,128,128]{4,3,2,1,0:T(8,128)(2,1)S(1)} %fusion.2), kind=kLoop, calls=%fused_computation | loop fusion | flops 6291456 | bytes 12582912 | tf_op jit(solution)/shard_map/stack | solution.py:80
  (2 shorter events, 0.0 us)
Async XLA Ops:
  12.0 6.4 %copy-start = (s32[3]{0:T(128)S(1)}, s32[3]{0:T(128)}, u32[]{:S(2)}) copy-start(s32[3]{0:T(128)} %param.4) | copy-start | bytes 40
  14.1 13.1 %all-to-all-start = ((bf16[8,2,128,128]{3,1,0,2:T(2,128)(2,1)}), bf16[8,2,128,128]{3,1,0,2:T(2,128)(2,1)S(1)}, u32[]{:S(2)}, u32[]{:S(2)}) async-start(bf16[8,2,128,128]{3,1,0,2:T(2,128)(2,1)} %copy.15), calls=%async_computation | async-start | bytes 1048576 | tf_op jit(solution)/shard_map/all_to_all | solution.py:62
  27.7 29.0 %collective-permute-start.2 = (bf16[32,2,32,128]{3,1,0,2:T(2,128)(2,1)S(1)}, bf16[32,2,32,128]{3,1,0,2:T(2,128)(2,1)S(1)}, u32[]{:S(2)}, u32[]{:S(2)}) collective-permute-start(bf16[32,2,32,128]{3,1,0,2:T(2,128)(2,1)S(1)} %bitcast.62), channel_id=1, source_target_pairs={{12,0},{16,4},{20,8},{24,12},{28,16},{13,1},{17,5},{21,9},{25,13},... | collective-permute-start | bytes 1572872 | tf_op jit(solution)/shard_map/ppermute | solution.py:18
  29.0 27.2 %collective-permute-start.1 = (bf16[32,2,32,128]{3,1,0,2:T(2,128)(2,1)S(1)}, bf16[32,2,32,128]{3,1,0,2:T(2,128)(2,1)S(1)}, u32[]{:S(2)}, u32[]{:S(2)}) collective-permute-start(bf16[32,2,32,128]{3,1,0,2:T(2,128)(2,1)S(1)} %bitcast.63), channel_id=1, source_target_pairs={{8,0},{12,4},{16,8},{20,12},{24,16},{28,20},{9,1},{13,5},{17,9},{2... | collective-permute-start | bytes 1572872 | tf_op jit(solution)/shard_map/ppermute | solution.py:18
  30.3 25.4 %collective-permute-start = (bf16[32,2,32,128]{3,1,0,2:T(2,128)(2,1)S(1)}, bf16[32,2,32,128]{3,1,0,2:T(2,128)(2,1)S(1)}, u32[]{:S(2)}, u32[]{:S(2)}) collective-permute-start(bf16[32,2,32,128]{3,1,0,2:T(2,128)(2,1)S(1)} %bitcast.64), channel_id=1, source_target_pairs={{4,0},{8,4},{12,8},{16,12},{20,16},{24,20},{28,24},{5,1},{9,5},{13... | collective-permute-start | bytes 1572872 | tf_op jit(solution)/shard_map/ppermute | solution.py:18
  31.6 70.2 %collective-permute-start.3 = (bf16[32,2,32,128]{3,1,0,2:T(2,128)(2,1)S(1)}, bf16[32,2,32,128]{3,1,0,2:T(2,128)(2,1)S(1)}, u32[]{:S(2)}, u32[]{:S(2)}) collective-permute-start(bf16[32,2,32,128]{3,1,0,2:T(2,128)(2,1)S(1)} %bitcast.65), channel_id=1, source_target_pairs={{16,0},{20,4},{24,8},{28,12},{17,1},{21,5},{25,9},{29,13},{18,2},{... | collective-permute-start | bytes 1572872 | tf_op jit(solution)/shard_map/ppermute | solution.py:18
where the time goes:
time: 110 us
  waiting for transfers between devices  66.6 us (61%)
  matrix products  10.6 us (10%)
  other arithmetic  10.2 us (9%)
  starting transfers between devices  9.58 us (9%)
  between operations  6.46 us (6%)
  local copies, waits for them, and re-layouts  6.39 us (6%)
    ppermute x4, waiting for transfers between devices, shifted(): return lax.ppermute(block, axis, route)  64.6 us
    dot_general x1, matrix products, shards(): jnp.einsum('cwt,tk->wkc', samples, table, preferred_element_type=jnp.floa...  7.15 us
    ppermute x4, starting transfers between devices, shifted(): return lax.ppermute(block, axis, route)  5.35 us
    another operation x1, other arithmetic  4.53 us
    all_to_all x1, starting transfers between devices, shards(): lax.all_to_all(whitened, 'win', split_axis=2, concat_axis=0, tiled=True)  4.24 us
    another operation x1, other arithmetic, shards(): cross_spectra = jnp.stack(results, axis=0)  3.15 us
    dot_general x3, matrix products, cross_pair(): lax.dot_general(left_side, right_side, (((1,), (0,)), ((2,), (1,))), pref...  2.8 us
  transfers between devices with their start and end apart: 5, of which 3 were waited for; matrix products, arithmetic and copies ran while one was open for 4% of the time, Pallas kernels for 0%

commit v1 on v0

--- a/solution.py
+++ b/solution.py
@@ -10,6 +10,28 @@
 OFFSET = 4
 water_level = 0.1
 epsilon = 1e-06
+
+
+def split_up(value, dim, devices):
+    before, after = (value.shape[:dim], value.shape[dim + 1 :])
+    return jnp.moveaxis(value.reshape(*before, devices, -1, *after), dim, 0)
+
+
+def laid_out(blocks, dim):
+    lengths = list(blocks.shape[1:])
+    lengths[dim] *= blocks.shape[0]
+    return jnp.moveaxis(blocks, 0, dim).reshape(lengths)
+
+
+def exchange_in_pairs(array, axis, split_dim, concat_dim):
+    length, index = (lax.axis_size(axis), lax.axis_index(axis))
+    blocks = split_up(array, split_dim, length)
+    outs = [blocks[index]]
+    for lap in range(1, length):
+        sent = blocks[index ^ lap]
+        outs.append(lax.ppermute(sent, axis, [(i, i ^ lap) for i in range(length)]))
+    blocks = jnp.stack(outs)[index ^ jnp.arange(length)]
+    return laid_out(blocks, concat_dim)
 
 
 def shifted(block, axis, distance):
@@ -59,7 +81,7 @@
     weights = band_weights()
     spectrum = jnp.einsum("cwt,tk->wkc", samples, table, preferred_element_type=jnp.float32)
     whitened = whiten_spectrum(spectrum.reshape(win_dev, 2, BINS, channels), weights)
-    by_bins = lax.all_to_all(whitened, "win", split_axis=2, concat_axis=0, tiled=True)
+    by_bins = exchange_in_pairs(whitened, "win", 2, 0)
     windows = by_bins.shape[0]
     bins_dev = by_bins.shape[2]
     swapped = jnp.stack([by_bins[:, 1], -by_bins[:, 0]], axis=1)

time: 110 us -> 106 us (0.964)
  waiting for transfers between devices: 66.6 us -> 63.2 us
    all_to_all x1 -> x0, starting transfers between devices: 4.24 us -> none  [shards(): lax.all_to_all(whitened, 'win', split_axis=2, concat_axis=0, tiled=True)]
    ppermute x0 -> x3, starting transfers between devices: none -> 3.15 us  [exchange_in_pairs(): outs.append(lax.ppermute(sent, axis, [(i, i ^ lap) for i in range(length)]))]
    all_to_all x1 -> x0, waiting for transfers between devices: 1.94 us -> none  [shards(): lax.all_to_all(whitened, 'win', split_axis=2, concat_axis=0, tiled=True)]
    ppermute x4, waiting for transfers between devices: 64.6 us -> 63.2 us  [shifted(): return lax.ppermute(block, axis, route)]
    convert_element_type x1 -> x0, local copies, waits for them, and re-layouts: 1.33 us -> none  [whiten_spectrum(): return (spectrum * factor[:, None]).astype(jnp.bfloat16)]
    gather x0 -> x2, local copies, waits for them, and re-layouts: none -> 1.2 us  [exchange_in_pairs(): blocks = jnp.stack(outs)[index ^ jnp.arange(length)]]
    another operation x1 -> x2, other arithmetic: 4.53 us -> 4.6 us
  transfers between devices with their start and end apart: 5 -> 7, of which waited for: 3 -> 2; matrix products, arithmetic and copies ran while one was open for 4% -> 5% of each run, Pallas kernels for 0% -> 0%
where the time goes in v1:
time: 106 us
  waiting for transfers between devices  63.2 us (60%)
  matrix products  10.6 us (10%)
  other arithmetic  10.4 us (10%)
  starting transfers between devices  8.5 us (8%)
  local copies, waits for them, and re-layouts  6.77 us (6%)
  between operations  6.66 us (6%)
    ppermute x4, waiting for transfers between devices, shifted(): return lax.ppermute(block, axis, route)  63.2 us
    dot_general x1, matrix products, shards(): jnp.einsum('cwt,tk->wkc', samples, table, preferred_element_type=jnp.floa...  7.16 us
    ppermute x4, starting transfers between devices, shifted(): return lax.ppermute(block, axis, route)  5.35 us
    another operation x1, other arithmetic  4.53 us
    another operation x1, other arithmetic, shards(): cross_spectra = jnp.stack(results, axis=0)  3.15 us
    ppermute x3, starting transfers between devices, exchange_in_pairs(): outs.append(lax.ppermute(sent, axis, [(i, i ^ lap) for i in range(length)]))  3.15 us
    dot_general x3, matrix products, cross_pair(): lax.dot_general(left_side, right_side, (((1,), (0,)), ((2,), (1,))), pref...  2.78 us
  transfers between devices with their start and end apart: 7, of which 2 were waited for; matrix products, arithmetic and copies ran while one was open for 5% of the time, Pallas kernels for 0%

profile of v1, /device:TPU:0, one launch (start us, length us, event | category | flops | bytes accessed | tf_op | source)
XLA Modules:
  0.0 106.1 jit_solution(10812640852230758182)
XLA Ops:
  0.0 0.1 convert_reduce_fusion
  0.1 0.1 multiply_subtract_fusion
  0.2 4.5 %multiply_convert_fusion.2 = (bf16[2048,128]{0,1:T(8,128)(2,1)S(1)}, bf16[2048,128]{0,1:T(8,128)(2,1)S(1)}) fusion(s32[128]{0:T(128)S(1)} %iota_add_fusion, f32[2048]{0:T(1024)S(1)} %get-tuple-element.19, f32[2048]{0:T(1024)S(1)} %get-tuple-element.20), kind=kLoop, calls=%fused_computation.25 | loop fusion | flops 4718592 | bytes 1065472 | tf_op jit(solution)/shard_map/convert
  4.7 7.2 %fusion = f32[256,128,8]{1,0,2:T(8,128)S(1)} fusion(bf16[128,8,2048]{2,1,0:T(8,128)(2,1)} %param.3, bf16[2048,128]{0,1:T(8,128)(2,1)S(1)} %get-tuple-element.18, bf16[2048,128]{0,1:T(8,128)(2,1)S(1)} %get-tuple-element.17), kind=kOutput, calls=%fused_computation.2 | convolution fusion | flops 1075838976 | bytes 6291456 | tf_op jit(solution)/shard_map/cwt,tk->wkc/dot_general | solution.py:82
  11.9 0.0 copy-start
  11.9 0.1 fusion.19
  12.0 0.6 fusion.6
  12.7 0.2 multiply_convert_fusion
  12.9 2.5 %collective-permute-start.2 = (bf16[8,2,32,128]{3,2,1,0:T(8,128)(2,1)S(1)}, bf16[8,2,32,128]{3,2,1,0:T(8,128)(2,1)S(1)}, u32[]{:S(2)}, u32[]{:S(2)}) collective-permute-start(bf16[8,2,32,128]{3,2,1,0:T(8,128)(2,1)S(1)} %get-tuple-element.11), channel_id=1, source_target_pairs={{0,3},{1,2},{2,1},{3,0},{4,7},{5,6},{6,5},{7,4},{8,11},{9,10},{10,... | collective-permute-start | bytes 393224 | tf_op jit(solution)/shard_map/ppermute | solution.py:32
  15.4 0.6 collective-permute-start.1
  16.0 0.0 collective-permute-start
  16.1 0.0 copy-done
  16.1 0.6 fusion.33
  23.1 0.0 collective-permute-done.2
  23.1 0.0 collective-permute-done.1
  23.1 0.0 collective-permute-done
  23.1 0.1 pad_maximum_fusion.2
  23.2 0.6 gather_fusion
  23.9 0.5 copy.11
  24.4 1.3 %collective-permute-start.4 = (bf16[32,2,32,128]{3,1,0,2:T(2,128)(2,1)S(1)}, bf16[32,2,32,128]{3,1,0,2:T(2,128)(2,1)S(1)}, u32[]{:S(2)}, u32[]{:S(2)}) collective-permute-start(bf16[32,2,32,128]{3,1,0,2:T(2,128)(2,1)S(1)} %copy.11), channel_id=1, source_target_pairs={{8,0},{12,4},{16,8},{20,12},{24,16},{28,20},{9,1},{13,5},{17,9},{2... | collective-permute-start | bytes 1572872 | tf_op jit(solution)/shard_map/ppermute | solution.py:40
  25.7 1.3 %collective-permute-start.3 = (bf16[32,2,32,128]{3,1,0,2:T(2,128)(2,1)S(1)}, bf16[32,2,32,128]{3,1,0,2:T(2,128)(2,1)S(1)}, u32[]{:S(2)}, u32[]{:S(2)}) collective-permute-start(bf16[32,2,32,128]{3,1,0,2:T(2,128)(2,1)S(1)} %copy.11), channel_id=1, source_target_pairs={{4,0},{8,4},{12,8},{16,12},{20,16},{24,20},{28,24},{5,1},{9,5},{13... | collective-permute-start | bytes 1572872 | tf_op jit(solution)/shard_map/ppermute | solution.py:40
  27.0 0.9 fusion.32
  28.0 1.2 %pad_maximum_fusion.3 = bf16[32,2,32,128]{3,1,0,2:T(2,128)(2,1)S(1)} fusion(bf16[32,1,32,128]{3,1,0,2:T(2,128)(2,1)S(1)} %get-tuple-element.9, bf16[32,1,32,128]{3,1,0,2:T(2,128)(2,1)S(1)} %get-tuple-element.8), kind=kLoop, calls=%fused_computation.36 | loop fusion | flops 1048576 | bytes 1048576 | tf_op jit(solution)/shard_map/stack | solution.py:87
  29.2 0.5 copy.10
  29.7 1.3 %collective-permute-start.5 = (bf16[32,2,32,128]{3,1,0,2:T(2,128)(2,1)S(1)}, bf16[32,2,32,128]{3,1,0,2:T(2,128)(2,1)S(1)}, u32[]{:S(2)}, u32[]{:S(2)}) collective-permute-start(bf16[32,2,32,128]{3,1,0,2:T(2,128)(2,1)S(1)} %copy.11), channel_id=1, source_target_pairs={{12,0},{16,4},{20,8},{24,12},{28,16},{13,1},{17,5},{21,9},{25,13},... | collective-permute-start | bytes 1572872 | tf_op jit(solution)/shard_map/ppermute | solution.py:40
  31.0 1.5 %collective-permute-start.6 = (bf16[32,2,32,128]{3,1,0,2:T(2,128)(2,1)S(1)}, bf16[32,2,32,128]{3,1,0,2:T(2,128)(2,1)S(1)}, u32[]{:S(2)}, u32[]{:S(2)}) collective-permute-start(bf16[32,2,32,128]{3,1,0,2:T(2,128)(2,1)S(1)} %copy.11), channel_id=1, source_target_pairs={{16,0},{20,4},{24,8},{28,12},{17,1},{21,5},{25,9},{29,13},{18,2},{... | collective-permute-start | bytes 1572872 | tf_op jit(solution)/shard_map/ppermute | solution.py:40
  32.5 0.5 copy_dynamic-update-slice_fusion
  33.1 20.1 %collective-permute-done.3 = bf16[32,2,32,128]{3,1,0,2:T(2,128)(2,1)S(1)} collective-permute-done((bf16[32,2,32,128]{3,1,0,2:T(2,128)(2,1)S(1)}, bf16[32,2,32,128]{3,1,0,2:T(2,128)(2,1)S(1)}, u32[]{:S(2)}, u32[]{:S(2)}) %collective-permute-start.3) | collective-permute-done | bytes 524320 | tf_op jit(solution)/shard_map/ppermute | solution.py:40
  53.2 0.5 bitcast_dynamic-update-slice_fusion.3
  53.7 0.0 collective-permute-done.4
  53.7 0.5 bitcast_dynamic-update-slice_fusion.2
  54.2 0.0 collective-permute-done.5
  54.2 0.5 bitcast_dynamic-update-slice_fusion.1
  54.7 43.1 %collective-permute-done.6 = bf16[32,2,32,128]{3,1,0,2:T(2,128)(2,1)S(1)} collective-permute-done((bf16[32,2,32,128]{3,1,0,2:T(2,128)(2,1)S(1)}, bf16[32,2,32,128]{3,1,0,2:T(2,128)(2,1)S(1)}, u32[]{:S(2)}, u32[]{:S(2)}) %collective-permute-start.6) | collective-permute-done | bytes 524320 | tf_op jit(solution)/shard_map/ppermute | solution.py:40
  97.8 0.5 bitcast_dynamic-update-slice_fusion
  98.3 1.8 %constant_dynamic-slice_fusion.2 = (bf16[1,32,2,32,128]{4,2,1,3,0:T(2,128)(2,1)S(1)}, bf16[1,32,2,32,128]{4,2,1,3,0:T(2,128)(2,1)S(1)}, bf16[1,32,2,32,128]{4,2,1,3,0:T(2,128)(2,1)S(1)}) fusion(bf16[5,32,2,32,128]{4,2,1,3,0:T(2,128)(2,1)S(1)} %bitcast_dynamic-update-slice_fusion, s32[]{:T(128)S(6)} %select_n.68, s32[]{:T(128)S(6)} %select_n.74, s32[]{:T(128)S(6)} %select_n.71), kind=kLoop, calls=%fused_computation.61 | loop fusion | bytes 3145740 | tf_op jit(solution)/shard_map/jit(dynamic_index_in_dim)/dynamic_slice | solution.py:97
  100.1 0.9 fusion.4
  101.1 0.9 fusion.2
  102.0 0.9 fusion.3
  103.0 3.2 %pad_maximum_fusion = bf16[3,32,2,128,128]{4,3,2,1,0:T(8,128)(2,1)} fusion(bf16[1,32,2,128,128]{4,3,2,1,0:T(8,128)(2,1)S(1)} %fusion.4, bf16[1,32,2,128,128]{4,3,2,1,0:T(8,128)(2,1)S(1)} %fusion.3, bf16[1,32,2,128,128]{4,3,2,1,0:T(8,128)(2,1)S(1)} %fusion.2), kind=kLoop, calls=%fused_computation.1 | loop fusion | flops 6291456 | bytes 12582912 | tf_op jit(solution)/shard_map/stack | solution.py:102
  (5 shorter events, 0.1 us)
Async XLA Ops:
  11.9 4.2 %copy-start = (s32[3]{0:T(128)S(1)}, s32[3]{0:T(128)}, u32[]{:S(2)}) copy-start(s32[3]{0:T(128)} %param.4) | copy-start | bytes 40
  12.9 10.2 %collective-permute-start.2 = (bf16[8,2,32,128]{3,2,1,0:T(8,128)(2,1)S(1)}, bf16[8,2,32,128]{3,2,1,0:T(8,128)(2,1)S(1)}, u32[]{:S(2)}, u32[]{:S(2)}) collective-permute-start(bf16[8,2,32,128]{3,2,1,0:T(8,128)(2,1)S(1)} %get-tuple-element.11), channel_id=1, source_target_pairs={{0,3},{1,2},{2,1},{3,0},{4,7},{5,6},{6,5},{7,4},{8,11},{9,10},{10,... | collective-permute-start | bytes 393224 | tf_op jit(solution)/shard_map/ppermute | solution.py:32
  15.4 7.7 %collective-permute-start.1 = (bf16[8,2,32,128]{3,2,1,0:T(8,128)(2,1)S(1)}, bf16[8,2,32,128]{3,2,1,0:T(8,128)(2,1)S(1)}, u32[]{:S(2)}, u32[]{:S(2)}) collective-permute-start(bf16[8,2,32,128]{3,2,1,0:T(8,128)(2,1)S(1)} %get-tuple-element.12), channel_id=1, source_target_pairs={{0,2},{1,3},{2,0},{3,1},{4,6},{5,7},{6,4},{7,5},{8,10},{9,11},{10,... | collective-permute-start | bytes 393224 | tf_op jit(solution)/shard_map/ppermute | solution.py:32
  16.0 7.1 %collective-permute-start = (bf16[8,2,32,128]{3,2,1,0:T(8,128)(2,1)S(1)}, bf16[8,2,32,128]{3,2,1,0:T(8,128)(2,1)S(1)}, u32[]{:S(2)}, u32[]{:S(2)}) collective-permute-start(bf16[8,2,32,128]{3,2,1,0:T(8,128)(2,1)S(1)} %get-tuple-element.13), channel_id=1, source_target_pairs={{0,1},{1,0},{2,3},{3,2},{4,5},{5,4},{6,7},{7,6},{8,9},{9,8},{10,11... | collective-permute-start | bytes 393224 | tf_op jit(solution)/shard_map/ppermute | solution.py:32
  24.4 29.2 %collective-permute-start.4 = (bf16[32,2,32,128]{3,1,0,2:T(2,128)(2,1)S(1)}, bf16[32,2,32,128]{3,1,0,2:T(2,128)(2,1)S(1)}, u32[]{:S(2)}, u32[]{:S(2)}) collective-permute-start(bf16[32,2,32,128]{3,1,0,2:T(2,128)(2,1)S(1)} %copy.11), channel_id=1, source_target_pairs={{8,0},{12,4},{16,8},{20,12},{24,16},{28,20},{9,1},{13,5},{17,9},{2... | collective-permute-start | bytes 1572872 | tf_op jit(solution)/shard_map/ppermute | solution.py:40
  25.7 27.4 %collective-permute-start.3 = (bf16[32,2,32,128]{3,1,0,2:T(2,128)(2,1)S(1)}, bf16[32,2,32,128]{3,1,0,2:T(2,128)(2,1)S(1)}, u32[]{:S(2)}, u32[]{:S(2)}) collective-permute-start(bf16[32,2,32,128]{3,1,0,2:T(2,128)(2,1)S(1)} %copy.11), channel_id=1, source_target_pairs={{4,0},{8,4},{12,8},{16,12},{20,16},{24,20},{28,24},{5,1},{9,5},{13... | collective-permute-start | bytes 1572872 | tf_op jit(solution)/shard_map/ppermute | solution.py:40
  29.7 24.4 %collective-permute-start.5 = (bf16[32,2,32,128]{3,1,0,2:T(2,128)(2,1)S(1)}, bf16[32,2,32,128]{3,1,0,2:T(2,128)(2,1)S(1)}, u32[]{:S(2)}, u32[]{:S(2)}) collective-permute-start(bf16[32,2,32,128]{3,1,0,2:T(2,128)(2,1)S(1)} %copy.11), channel_id=1, source_target_pairs={{12,0},{16,4},{20,8},{24,12},{28,16},{13,1},{17,5},{21,9},{25,13},... | collective-permute-start | bytes 1572872 | tf_op jit(solution)/shard_map/ppermute | solution.py:40
  31.0 66.8 %collective-permute-start.6 = (bf16[32,2,32,128]{3,1,0,2:T(2,128)(2,1)S(1)}, bf16[32,2,32,128]{3,1,0,2:T(2,128)(2,1)S(1)}, u32[]{:S(2)}, u32[]{:S(2)}) collective-permute-start(bf16[32,2,32,128]{3,1,0,2:T(2,128)(2,1)S(1)} %copy.11), channel_id=1, source_target_pairs={{16,0},{20,4},{24,8},{28,12},{17,1},{21,5},{25,9},{29,13},{18,2},{... | collective-permute-start | bytes 1572872 | tf_op jit(solution)/shard_map/ppermute | solution.py:40
